TPU v7x, 128 devices: a whole 4x4x4 slice. The times are simulated.
128 devices in a mesh: slab: 4 (over z), ang: 32 (over x, y, core).
Axes of the slice: x: 4, y: 4, z: 4, core: 2. Of those that a mesh axis runs over, the one named last changes fastest.
Arguments:
- object_slices: float32 [2, 1024, 128, 128], P(None, ('slab', 'ang')), may hold values from -6 to 6
- views: float32 [2, 1024, 32, 128], P(None, 'slab', 'ang'), may hold values from -6 to 6
- scaled_dual: float32 [2, 1024, 32, 128], P(None, 'slab', 'ang'), may hold values from -6 to 6
- probe: float32 [2, 128, 128], replicated, may hold values from -3 to 3
- intensities: bfloat16 [32, 48, 128, 128], P('ang', 'slab'), may hold values from 0 to 2
- tile_rows: int32 [32, 48], P('ang', 'slab'), may hold values from 0 to 15
- live_counts: int32 [32, 4], P('ang', 'slab'), may hold values from 1 to 12, as said below
Outputs:
- object_new: float32 [2, 1024, 128, 128], P(None, ('slab', 'ang'))
- views_new: float32 [2, 1024, 32, 128], P(None, 'slab', 'ang')
- dual_new: float32 [2, 1024, 32, 128], P(None, 'slab', 'ang')
- probe_new: float32 [2, 128, 128], replicated
Inputs may be any that keep to these rules, and one draw needn't show every extreme that they name: `tile_rows`: a slot's patch starts 16 times this value rows into its slab and may reach 112 rows into the next slab. `live_counts`: slots at and past the count of their angle and slab carry no data; some angle and slab have all 12 slots live.
All inputs are finite; a program needn't handle non-finite values.
Results may differ from a plain program's by a relative error of at most 0.0028.
The roundings to bfloat16 on the way count: a program that leaves them out, or rounds other values in their place, can miss the bound.
Values sent between devices are 32-bit elements; how exact they have to be, the bound alone decides.
A program may use at most 64 MiB of HBM per device.

v0:
```python
import math

import jax
import jax.numpy as jnp
import ml_dtypes
import numpy as np
from jax import lax
from jax.experimental import pallas as pl
from jax.experimental.pallas import tpu as pltpu
from jax.sharding import PartitionSpec as P

SIDE = 128
HALF = SIDE // 2
STEP = 16
ANGLES = 32
SLICE_DEV = 8
ROWS = ANGLES * SLICE_DEV
CAP = 12
BATCH = 4
HALO = SIDE - STEP
N_SLAB = 4
QUARTER = ANGLES // 2

view_rate = 0.1
probe_rate = 16.0
epsilon = 1e-06

F32 = jnp.float32
BF16 = jnp.bfloat16
MESH = pl.DeviceIdType.MESH

GROUPS = [(0, 1), (2, 3), (4, 5), (6, 7), (8, 9), (10, 11), (12, 13), (14, 15), (16,)]
REACH = [16, 32, 32, 48, 64, 64, 64, 64, 64]


def dft_tables():
    counter = np.arange(SIDE)
    product = (counter[:, None] * counter[None, :] % SIDE).astype(np.float32)
    angle = product * np.float32(2.0 * math.pi / SIDE)
    factor = np.float32(1.0 / math.sqrt(SIDE))
    return (np.cos(angle) * factor).astype(np.float32), (np.sin(angle) * factor).astype(np.float32)


def split_table(table):
    high = table.astype(ml_dtypes.bfloat16)
    low = (table - high.astype(np.float32)).astype(ml_dtypes.bfloat16)
    return np.stack([high, low])


def hat(position):
    cells = np.arange(SIDE)[:, None] - HALF
    distance = np.abs(cells - position[None, :])
    return np.maximum(0.0, 1.0 - np.minimum(distance, SIDE - distance))


def tables():
    cosine, sine = dft_tables()
    shift_c, shift_s = np.roll(cosine, HALF, axis=0), np.roll(sine, HALF, axis=0)
    right = np.block([[shift_c.T, -shift_s.T], [shift_s.T, shift_c.T]])
    left = np.ascontiguousarray(right.T)
    sign = (1 - 2 * (np.arange(SIDE) % 2)).astype(np.float32)[None, :]
    to_view = np.block([[cosine * sign, sine * sign], [-sine * sign, cosine * sign]])
    half_left = np.block([[cosine, sine], [-sine, cosine]]).astype(ml_dtypes.bfloat16)
    half_right = np.block([[cosine, -sine], [sine, cosine]]).astype(ml_dtypes.bfloat16)
    radius = np.arange(SIDE) - HALF
    along = np.zeros((len(GROUPS), 2, SIDE, 2 * SIDE), np.float32)
    across = np.zeros((len(GROUPS), SIDE, 2 * SIDE), np.float32)
    for g, members in enumerate(GROUPS):
        for i, b in enumerate(members):
            lanes = slice(i * SIDE, (i + 1) * SIDE)
            row = radius * math.sin(math.pi * b / ANGLES)
            along[g, 0, :, lanes] = hat(row)
            if 0 < b < QUARTER:
                along[g, 1, :, lanes] = hat(-row)
            across[g, :, lanes] = hat(radius * math.cos(math.pi * b / ANGLES))
    return dict(
        right=split_table(right),
        left=split_table(left),
        to_view=split_table(to_view),
        to_line=np.ascontiguousarray(to_view.T).astype(ml_dtypes.bfloat16),
        half=np.stack([half_left, half_right]),
        along=along,
        along16=along.astype(ml_dtypes.bfloat16),
        across=np.concatenate([across, across], axis=1).astype(ml_dtypes.bfloat16),
        spread=np.ascontiguousarray(np.swapaxes(across, 1, 2)).astype(ml_dtypes.bfloat16),
    )


TABLE_NAMES = ["right", "left", "to_view", "to_line", "half", "along", "along16", "across", "spread"]


def dot(a, b):
    return jnp.dot(a, b, preferred_element_type=F32)


def split(x):
    high = x.astype(BF16)
    return high, (x - high.astype(F32)).astype(BF16)


def beside(x):
    return jnp.concatenate([x[: x.shape[0] // 2], x[x.shape[0] // 2 :]], axis=1)


def stacked(x):
    return jnp.concatenate([x[:, : x.shape[1] // 2], x[:, x.shape[1] // 2 :]], axis=0)


def spectrum(obj, t, out):
    def pair(i, carry):
        rows = [jnp.concatenate([obj[0, 2 * i + z], obj[1, 2 * i + z]], axis=1) for z in range(2)]
        high, low = split(jnp.concatenate(rows, axis=0))
        half = dot(high, t["right"][0]) + dot(low, t["right"][0]) + dot(high, t["right"][1])
        cols = jnp.concatenate([stacked(half[:SIDE]), stacked(half[SIDE:])], axis=1)
        high, low = split(cols)
        full = dot(t["left"][0], high) + dot(t["left"][0], low) + dot(t["left"][1], high)
        high, low = split(full)
        for z in range(2):
            for c in range(2):
                rows, lanes = slice(c * SIDE, (c + 1) * SIDE), slice(z * SIDE, (z + 1) * SIDE)
                out[c, 2 * i + z, :, :SIDE] = high[rows, lanes]
                out[c, 2 * i + z, :, SIDE:] = low[rows, lanes]
        return carry

    lax.fori_loop(0, SLICE_DEV // 2, pair, 0)


def sample(plane, c, t, put):
    depth = plane.shape[-1]
    for g, members in enumerate(GROUPS):
        lanes = len(members) * SIDE
        low, top = HALF - REACH[g], HALF + REACH[g]
        sums = [[], []]
        for z in range(SLICE_DEV):
            rows = dot(plane[c, z, low:top, :], t["across"][g, :depth, :lanes])
            for side in range(len(members)):
                weighed = rows * t["along"][g, side, low:top, :lanes]
                sums[side].append(jnp.sum(weighed, axis=0, keepdims=True))
        for side in range(len(members)):
            whole = jnp.concatenate(sums[side], axis=0)
            for i, b in enumerate(members):
                if side == 0 or b > 0:
                    put(c, QUARTER - b if side == 0 else QUARTER + b, whole[:, i * SIDE : (i + 1) * SIDE])


def spread(lines, c, t, out):
    for z in range(SLICE_DEV):
        total = None
        for g, members in enumerate(GROUPS):
            lanes = len(members) * SIDE
            low, top = HALF - REACH[g], HALF + REACH[g]
            terms = None
            for side in range(len(members)):
                picks = [lines[c, (QUARTER - b) if side == 0 else (QUARTER + b), z : z + 1, :] for b in members]
                line = jnp.concatenate(picks, axis=1).astype(BF16)
                term = t["along16"][g, side, low:top, :lanes] * line
                terms = term if terms is None else terms + term
            part = dot(terms, t["spread"][g, :lanes, :])
            if total is None:
                total = part
            else:
                edge = (part.shape[0] - total.shape[0]) // 2
                if edge:
                    total = jnp.concatenate(
                        [part[:edge], part[edge : edge + total.shape[0]] + total, part[edge + total.shape[0] :]], axis=0
                    )
                else:
                    total = part + total
        out[c, z] = total.astype(BF16)


def lines_to_views(lines, t, put):
    joined = jnp.concatenate([lines[0].reshape(ROWS, SIDE), lines[1].reshape(ROWS, SIDE)], axis=1)
    high, low = split(joined)
    result = dot(high, t["to_view"][0]) + dot(low, t["to_view"][0]) + dot(high, t["to_view"][1])
    for c in range(2):
        put(c, result[:, c * SIDE : (c + 1) * SIDE].reshape(ANGLES, SLICE_DEV, SIDE))


def correction(grid, t, put):
    def pair(i, carry):
        rows = [jnp.concatenate([grid[0, 2 * i + z], grid[1, 2 * i + z]], axis=1) for z in range(2)]
        half = dot(jnp.concatenate(rows, axis=0), t["left"][0]).astype(BF16)
        cols = jnp.concatenate([stacked(half[:SIDE]), stacked(half[SIDE:])], axis=1)
        full = dot(t["right"][0], cols) * (1.0 / ANGLES)
        for z in range(2):
            for c in range(2):
                put(c, 2 * i + z, full[c * SIDE : (c + 1) * SIDE, z * SIDE : (z + 1) * SIDE])
        return carry

    lax.fori_loop(0, SLICE_DEV // 2, pair, 0)


def patches(extended, probe, measured, starts, count, t, grads, probe_grad, power):
    probe_re, probe_im = probe[0], probe[1]
    edge = jnp.zeros((2, STEP, SIDE), F32)
    for first in range(0, CAP, BATCH):
        slots = range(first, first + BATCH)
        exits = []
        for n in slots:
            re = extended[0, pl.ds(starts[n], SIDE), :]
            im = extended[1, pl.ds(starts[n], SIDE), :]
            exits.append(jnp.concatenate([probe_re * re - probe_im * im, probe_re * im + probe_im * re], axis=0).astype(BF16))
        half = dot(t["half"][0], jnp.concatenate(exits, axis=1)).astype(BF16)
        field = dot(
            jnp.concatenate([beside(half[:, i * SIDE : (i + 1) * SIDE]) for i in range(BATCH)], axis=0), t["half"][1]
        )
        pulls = []
        for i, n in enumerate(slots):
            field_re = field[i * SIDE : (i + 1) * SIDE, :SIDE]
            field_im = field[i * SIDE : (i + 1) * SIDE, SIDE:]
            live = jnp.where(n < count, 1.0, 0.0).astype(F32)
            misfit = (field_re * field_re + field_im * field_im - measured[n].astype(F32)) * live
            pulls.append(jnp.concatenate([field_re * misfit, field_im * misfit], axis=0).astype(BF16))
        half = dot(t["half"][1], jnp.concatenate(pulls, axis=1)).astype(BF16)
        back = dot(
            jnp.concatenate([beside(half[:, i * SIDE : (i + 1) * SIDE]) for i in range(BATCH)], axis=0), t["half"][0]
        )
        sum_re = sum_im = squares = None
        for i, n in enumerate(slots):
            re = extended[0, pl.ds(starts[n], SIDE), :]
            im = extended[1, pl.ds(starts[n], SIDE), :]
            live = jnp.where(n < count, 1.0, 0.0).astype(F32)
            back_re = back[i * SIDE : (i + 1) * SIDE, :SIDE]
            back_im = back[i * SIDE : (i + 1) * SIDE, SIDE:]
            grads[n, 0, STEP : STEP + SIDE, :] = probe_re * back_re + probe_im * back_im
            grads[n, 1, STEP : STEP + SIDE, :] = probe_re * back_im - probe_im * back_re
            grads[n, :, :STEP, :] = edge
            grads[n, :, STEP + SIDE :, :] = edge
            term_re = re * back_re + im * back_im
            term_im = re * back_im - im * back_re
            square = jnp.sum((re * re + im * im).reshape(SIDE // 8, 8, SIDE), axis=0) * live
            sum_re = term_re if sum_re is None else sum_re + term_re
            sum_im = term_im if sum_im is None else sum_im + term_im
            squares = square if squares is None else squares + square
        if first:
            probe_grad[0] += sum_re
            probe_grad[1] += sum_im
            power[...] += squares
        else:
            probe_grad[0] = sum_re
            probe_grad[1] = sum_im
            power[...] = squares


def kernel(obj, views, dual, probe, measured, tiles, count, *rest):
    t = dict(zip(TABLE_NAMES, rest))
    rest = rest[len(TABLE_NAMES) :]
    obj_out, views_out, dual_out, probe_out = rest[:4]
    (
        extended, halo, grads, probe_grad, power, grad_out, grad_in, target, spec, lines, back, grid,
        came, now_send, now_came, after_send, after_came, chunk_send, chunk_came, slab_send, slab_came,
        halo_sem, grad_sem, target_sem, now_sem, after_sem, chunk_sem, slab_sem, gather_sem,
    ) = rest[4:]
    slab, ang = lax.axis_index("slab"), lax.axis_index("ang")

    def ang_peer(k):
        return lax.rem(ang + k, ANGLES)

    def slab_peer(k):
        return lax.rem(slab + k, N_SLAB)

    def each_ang(body):
        def step(k, carry):
            body(ang_peer(k))
            return carry

        lax.fori_loop(1, ANGLES, step, 0)

    def remote(src, dst, sems, to):
        return pltpu.make_async_remote_copy(
            src_ref=src, dst_ref=dst, send_sem=sems.at[0], recv_sem=sems.at[1], device_id=to, device_id_type=MESH
        )

    def block(ref, p):
        return ref.at[:, pl.ds(pl.multiple_of(p * SLICE_DEV, SLICE_DEV), SLICE_DEV), :]

    def await_bytes(ref, sem):
        pltpu.make_async_copy(ref, ref, sem).wait()

    barrier = pltpu.get_barrier_semaphore()
    each_ang(lambda p: pl.semaphore_signal(barrier, inc=1, device_id=(slab, p), device_id_type=MESH))
    for k in range(1, N_SLAB):
        pl.semaphore_signal(barrier, inc=1, device_id=(slab_peer(k), ang), device_id_type=MESH)
    pl.semaphore_wait(barrier, ANGLES - 1 + N_SLAB - 1)

    halo_copy = remote(views.at[:, :HALO, :], halo, halo_sem, (slab_peer(N_SLAB - 1), ang))
    halo_copy.start()
    spectrum(obj, t, spec)
    extended[:, : ROWS, :] = views[...]
    halo_copy.wait()
    inner = jnp.where(slab < N_SLAB - 1, 1.0, 0.0).astype(F32)
    extended[:, ROWS:, :] = halo[...] * inner

    picked = [tiles[0, n] for n in range(CAP)]
    starts = [tile * STEP for tile in picked]
    patches(extended, probe, measured, starts, count[0, 0], t, grads, probe_grad, power)

    def gathered(r):
        sums = [None, None]
        for n in range(CAP):
            at = (lax.max(lax.min(r - picked[n], SIDE // STEP), -1) + 1) * STEP
            for c in range(2):
                piece = grads[n, c, pl.ds(at, STEP), :]
                sums[c] = piece if sums[c] is None else sums[c] + piece
        return sums

    def outer(r, carry):
        sums = gathered(r + ROWS // STEP)
        for c in range(2):
            grad_out[c, pl.ds(pl.multiple_of(r * STEP, STEP), STEP), :] = sums[c]
        return carry

    lax.fori_loop(0, HALO // STEP, outer, 0)
    grad_copy = remote(grad_out, grad_in, grad_sem, (slab_peer(1), ang))
    grad_copy.start()

    def inside(r, carry):
        sums = gathered(r)
        at = pl.ds(pl.multiple_of(r * STEP, STEP), STEP)
        for c in range(2):
            target[c, at, :] = (1.0 - view_rate) * (views[c, at, :] + dual[c, at, :]) - view_rate * sums[c]
        return carry

    lax.fori_loop(0, ROWS // STEP, inside, 0)

    def send_target(p):
        remote(block(target, p), came.at[ang], target_sem, (slab, p)).start()

    ready = HALO // SLICE_DEV
    each_ang(lambda p: pl.when(p >= ready)(lambda: send_target(p)))

    for c in range(2):
        for i in range(SIDE // 8):
            chunk_send[c * (SIDE // 8) + i, :8, :] = probe_grad[c, 8 * i : 8 * i + 8, :]
            chunk_send[c * (SIDE // 8) + i, 8:, :] = power[...]
    grad_copy.wait()
    from_above = jnp.where(slab > 0, view_rate, 0.0).astype(F32)
    target[:, :HALO, :] = target[:, :HALO, :] - from_above * grad_in[...]
    each_ang(lambda p: pl.when(p < ready)(lambda: send_target(p)))
    came[ang] = target[:, pl.ds(pl.multiple_of(ang * SLICE_DEV, SLICE_DEV), SLICE_DEV), :]
    each_ang(lambda p: remote(chunk_send.at[p], chunk_came.at[ang], chunk_sem, (slab, p)).start())
    chunk_came[ang] = chunk_send[ang]

    def put_line(c, a, samples):
        lines[c, a] = samples

    def sample_now(c, carry):
        sample(spec, c, t, put_line)
        return carry

    lax.fori_loop(0, 2, sample_now, 0)

    def put_now(c, value):
        now_send[:, c] = value

    lines_to_views(lines, t, put_now)
    each_ang(lambda p: remote(now_send.at[p], block(now_came, ang), now_sem, (slab, p)).start())
    now_came[:, pl.ds(pl.multiple_of(ang * SLICE_DEV, SLICE_DEV), SLICE_DEV), :] = now_send[ang]

    await_bytes(chunk_came.at[: ANGLES - 1], chunk_sem.at[1])
    total = jnp.sum(chunk_came[...], axis=0)
    slab_send[...] = total
    for k in range(1, N_SLAB):
        remote(slab_send, slab_came.at[slab], slab_sem, (slab_peer(k), ang)).start()
    slab_came[slab] = total

    await_bytes(came.at[: ANGLES - 1], target_sem.at[1])
    joined = jnp.concatenate([came[:, c].reshape(ROWS, SIDE) for c in range(2)], axis=1).astype(BF16)
    pulled = dot(joined, t["to_line"][...])
    for c in range(2):
        back[c] = (1.0 - view_rate) * lines[c] - pulled[:, c * SIDE : (c + 1) * SIDE].reshape(ANGLES, SLICE_DEV, SIDE)

    def put_after(c, a, samples):
        lines[c, a] = lines[c, a] - samples * (1.0 / ANGLES)

    def sample_after(c, carry):
        spread(back, c, t, grid)
        sample(grid, c, t, put_after)
        return carry

    lax.fori_loop(0, 2, sample_after, 0)

    def put_views(c, value):
        after_send[:, c] = value

    lines_to_views(lines, t, put_views)
    each_ang(lambda p: remote(after_send.at[p], block(after_came, ang), after_sem, (slab, p)).start())
    after_came[:, pl.ds(pl.multiple_of(ang * SLICE_DEV, SLICE_DEV), SLICE_DEV), :] = after_send[ang]

    await_bytes(slab_came.at[: N_SLAB - 1], slab_sem.at[1])
    total = jnp.sum(slab_came[...], axis=0)
    scale = probe_rate / (jnp.sum(total[8:]) * (1.0 / (SIDE * SIDE)) + epsilon)
    mine = pl.ds(pl.multiple_of(ang * 8, 8), 8)
    probe_out[mine, :] = probe.reshape(2 * SIDE, SIDE)[mine, :] - total[:8] * scale
    each_ang(lambda p: remote(probe_out.at[mine, :], probe_out.at[mine, :], gather_sem, (slab, p)).start())

    def put_object(c, z, value):
        obj_out[c, z] = obj[c, z] - value

    correction(grid, t, put_object)

    await_bytes(block_span(now_came), now_sem.at[1])
    views_out[...] = target[...] - dual[...] + view_rate * now_came[...]
    await_bytes(block_span(after_came), after_sem.at[1])
    dual_out[...] = target[...] + view_rate * now_came[...] - after_came[...]
    await_bytes(probe_out.at[: 8 * (ANGLES - 1), :], gather_sem.at[1])

    await_bytes(came.at[: ANGLES - 1], target_sem.at[0])
    await_bytes(now_send.at[: ANGLES - 1], now_sem.at[0])
    await_bytes(after_send.at[: ANGLES - 1], after_sem.at[0])
    await_bytes(chunk_send.at[: ANGLES - 1], chunk_sem.at[0])
    await_bytes(slab_came.at[: N_SLAB - 1], slab_sem.at[0])
    await_bytes(probe_out.at[: 8 * (ANGLES - 1), :], gather_sem.at[0])


def block_span(ref):
    return ref.at[:, : SLICE_DEV * (ANGLES - 1), :]


def body(object_slices, views, scaled_dual, probe, intensities, tile_rows, live_counts):
    table = tables()
    args = [
        object_slices,
        views.reshape(2, ROWS, SIDE),
        scaled_dual.reshape(2, ROWS, SIDE),
        probe,
        intensities.reshape(CAP, SIDE, SIDE),
        tile_rows,
        live_counts,
    ] + [jnp.asarray(table[name]) for name in TABLE_NAMES]
    vmem, smem = pl.BlockSpec(memory_space=pltpu.VMEM), pl.BlockSpec(memory_space=pltpu.SMEM)
    blocks = (ANGLES, 2, SLICE_DEV, SIDE)
    dma = pltpu.SemaphoreType.DMA((2,))
    obj_new, views_new, dual_new, probe_new = pl.pallas_call(
        kernel,
        out_shape=[
            jax.ShapeDtypeStruct(object_slices.shape, F32),
            jax.ShapeDtypeStruct((2, ROWS, SIDE), F32),
            jax.ShapeDtypeStruct((2, ROWS, SIDE), F32),
            jax.ShapeDtypeStruct((2 * SIDE, SIDE), F32),
        ],
        in_specs=[vmem] * 5 + [smem] * 2 + [vmem] * len(TABLE_NAMES),
        out_specs=[vmem] * 4,
        scratch_shapes=[
            pltpu.VMEM((2, ROWS + HALO, SIDE), F32),
            pltpu.VMEM((2, HALO, SIDE), F32),
            pltpu.VMEM((CAP, 2, SIDE + 2 * STEP, SIDE), F32),
            pltpu.VMEM((2, SIDE, SIDE), F32),
            pltpu.VMEM((8, SIDE), F32),
            pltpu.VMEM((2, HALO, SIDE), F32),
            pltpu.VMEM((2, HALO, SIDE), F32),
            pltpu.VMEM((2, ROWS, SIDE), F32),
            pltpu.VMEM((2, SLICE_DEV, SIDE, 2 * SIDE), BF16),
            pltpu.VMEM((2, ANGLES, SLICE_DEV, SIDE), F32),
            pltpu.VMEM((2, ANGLES, SLICE_DEV, SIDE), F32),
            pltpu.VMEM((2, SLICE_DEV, SIDE, SIDE), BF16),
            pltpu.VMEM(blocks, F32),
            pltpu.VMEM(blocks, F32),
            pltpu.VMEM((2, ROWS, SIDE), F32),
            pltpu.VMEM(blocks, F32),
            pltpu.VMEM((2, ROWS, SIDE), F32),
            pltpu.VMEM((ANGLES, 16, SIDE), F32),
            pltpu.VMEM((ANGLES, 16, SIDE), F32),
            pltpu.VMEM((16, SIDE), F32),
            pltpu.VMEM((N_SLAB, 16, SIDE), F32),
        ]
        + [dma] * 8,
        compiler_params=pltpu.CompilerParams(collective_id=0, has_side_effects=True, vmem_limit_bytes=48 * 1024 * 1024),
    )(*args)
    return (
        obj_new,
        views_new.reshape(views.shape),
        dual_new.reshape(scaled_dual.shape),
        probe_new.reshape(probe.shape),
    )


def solution(mesh):
    in_specs = (
        P(None, ("slab", "ang"), None, None),
        P(None, "slab", "ang", None),
        P(None, "slab", "ang", None),
        P(),
        P("ang", "slab", None, None),
        P("ang", "slab"),
        P("ang", "slab"),
    )
    out_specs = (
        P(None, ("slab", "ang"), None, None),
        P(None, "slab", "ang", None),
        P(None, "slab", "ang", None),
        P(),
    )
    return jax.shard_map(body, mesh=mesh, in_specs=in_specs, out_specs=out_specs, check_vma=False)
```

profile of v0, /device:TPU:1, one launch (start us, length us, event | category | flops | bytes accessed | tf_op | source)
XLA Modules:
  0.0 60.6 jit_solution(6633875259853593798)
XLA Ops:
  1.3 0.0 copy-start
  1.3 1.2 %copy-done = f32[2,8,128,128]{3,2,1,0:T(8,128)S(1)} copy-done((f32[2,8,128,128]{3,2,1,0:T(8,128)S(1)}, f32[2,8,128,128]{3,2,1,0:T(8,128)}, u32[]{:S(2)}) %copy-start) | copy-done | bytes 1048600
  2.5 0.0 copy-start.1
  2.5 1.1 %copy-done.1 = bf16[9,256,128]{2,1,0:T(8,128)(2,1)S(1)} copy-done((bf16[9,256,128]{2,1,0:T(8,128)(2,1)S(1)}, bf16[9,256,128]{2,1,0:T(8,128)(2,1)}, u32[]{:S(2)}) %copy-start.1) | copy-done | bytes 589848
  3.6 0.0 copy-start.2
  3.6 1.0 %copy-done.2 = bf16[1,12,128,128]{3,2,1,0:T(8,128)(2,1)S(1)} copy-done((bf16[1,12,128,128]{3,2,1,0:T(8,128)(2,1)S(1)}, bf16[1,12,128,128]{3,2,1,0:T(8,128)(2,1)}, u32[]{:S(2)}) %copy-start.2) | copy-done | bytes 393240
  4.6 0.0 copy-start.3
  4.6 0.9 %copy-done.3 = f32[2,256,1,128]{3,2,1,0:T(1,128)S(1)} copy-done((f32[2,256,1,128]{3,2,1,0:T(1,128)S(1)}, f32[2,256,1,128]{3,2,1,0:T(1,128)}, u32[]{:S(2)}) %copy-start.3) | copy-done | bytes 262168
  5.5 0.0 copy-start.4
  5.5 0.9 %copy-done.4 = f32[2,256,1,128]{3,2,1,0:T(1,128)S(1)} copy-done((f32[2,256,1,128]{3,2,1,0:T(1,128)S(1)}, f32[2,256,1,128]{3,2,1,0:T(1,128)}, u32[]{:S(2)}) %copy-start.4) | copy-done | bytes 262168
  6.5 0.0 copy-start.5
  6.5 0.9 %copy-done.5 = bf16[2,256,256]{2,1,0:T(8,128)(2,1)S(1)} copy-done((bf16[2,256,256]{2,1,0:T(8,128)(2,1)S(1)}, bf16[2,256,256]{2,1,0:T(8,128)(2,1)}, u32[]{:S(2)}) %copy-start.5) | copy-done | bytes 262168
  7.4 0.0 copy-start.6
  7.4 0.9 %copy-done.6 = bf16[2,256,256]{2,1,0:T(8,128)(2,1)S(1)} copy-done((bf16[2,256,256]{2,1,0:T(8,128)(2,1)S(1)}, bf16[2,256,256]{2,1,0:T(8,128)(2,1)}, u32[]{:S(2)}) %copy-start.6) | copy-done | bytes 262168
  8.4 0.0 copy-start.7
  8.4 0.9 %copy-done.7 = bf16[2,256,256]{2,1,0:T(8,128)(2,1)S(1)} copy-done((bf16[2,256,256]{2,1,0:T(8,128)(2,1)S(1)}, bf16[2,256,256]{2,1,0:T(8,128)(2,1)}, u32[]{:S(2)}) %copy-start.7) | copy-done | bytes 262168
  9.3 0.0 copy-start.8
  9.3 0.9 %copy-done.8 = bf16[2,256,256]{2,1,0:T(8,128)(2,1)S(1)} copy-done((bf16[2,256,256]{2,1,0:T(8,128)(2,1)S(1)}, bf16[2,256,256]{2,1,0:T(8,128)(2,1)}, u32[]{:S(2)}) %copy-start.8) | copy-done | bytes 262168
  10.3 0.0 copy-start.9
  10.3 0.9 %copy-done.9 = f32[2,128,128]{2,1,0:T(8,128)S(1)} copy-done((f32[2,128,128]{2,1,0:T(8,128)S(1)}, f32[2,128,128]{2,1,0:T(8,128)}, u32[]{:S(2)}) %copy-start.9) | copy-done | bytes 131096
  11.2 0.0 copy-start.10
  11.2 0.9 %copy-done.10 = bf16[256,256]{1,0:T(8,128)(2,1)S(1)} copy-done((bf16[256,256]{1,0:T(8,128)(2,1)S(1)}, bf16[256,256]{1,0:T(8,128)(2,1)}, u32[]{:S(2)}) %copy-start.10) | copy-done | bytes 131096
  12.1 0.0 copy-start.11
  12.1 0.7 %copy-done.11 = s32[1,12]{1,0:T(1,128)S(1)} copy-done((s32[1,12]{1,0:T(1,128)S(1)}, s32[1,12]{1,0:T(1,128)}, u32[]{:S(2)}) %copy-start.11) | copy-done | bytes 72
  12.7 44.8 %shard_map.183 = (f32[2,8,128,128]{3,2,1,0:T(8,128)S(1)}, f32[2,256,128]{2,1,0:T(8,128)S(1)}, f32[2,256,128]{2,1,0:T(8,128)S(1)}, f32[256,128]{1,0:T(8,128)S(1)}) custom-call(f32[2,8,128,128]{3,2,1,0:T(8,128)S(1)} %copy-done, f32[2,256,128]{2,1,0:T(8,128)S(1)} %bitcast.11, f32[2,256,128]{2,1,0:T(8,128)S(1)} %bitcast.12, f32[2,128,128]{2,1,0:T(8,128)S(1)} %copy-done.9, ...), custom_call_target="tpu_custom_call" | custom-call | tf_op jit(solution)/shard_map/pallas_call | solution.py:435
  57.6 1.0 %copy.27 = f32[2,8,128,128]{3,2,1,0:T(8,128)} copy(f32[2,8,128,128]{3,2,1,0:T(8,128)S(1)} %get-tuple-element.20) | data formatting | bytes 2097152
  58.6 0.7 %copy.28 = f32[2,256,1,128]{3,2,1,0:T(1,128)} copy(f32[2,256,1,128]{3,2,1,0:T(1,128)S(1)} %bitcast.14) | data formatting | bytes 524288
  59.3 0.7 %copy.29 = f32[2,256,1,128]{3,2,1,0:T(1,128)} copy(f32[2,256,1,128]{3,2,1,0:T(1,128)S(1)} %bitcast.13) | data formatting | bytes 524288
  60.0 0.7 %copy.30 = f32[2,128,128]{2,1,0:T(8,128)} copy(f32[2,128,128]{2,1,0:T(8,128)S(1)} %bitcast.15) | data formatting | bytes 262144
Async XLA Ops:
  1.3 1.2 %copy-start = (f32[2,8,128,128]{3,2,1,0:T(8,128)S(1)}, f32[2,8,128,128]{3,2,1,0:T(8,128)}, u32[]{:S(2)}) copy-start(f32[2,8,128,128]{3,2,1,0:T(8,128)} %obj.1) | copy-start | bytes 3145732
  2.5 1.1 %copy-start.1 = (bf16[9,256,128]{2,1,0:T(8,128)(2,1)S(1)}, bf16[9,256,128]{2,1,0:T(8,128)(2,1)}, u32[]{:S(2)}) copy-start(bf16[9,256,128]{2,1,0:T(8,128)(2,1)} %constant.26.clone.rest_8_) | copy-start | bytes 1769476
  3.6 1.0 %copy-start.2 = (bf16[1,12,128,128]{3,2,1,0:T(8,128)(2,1)S(1)}, bf16[1,12,128,128]{3,2,1,0:T(8,128)(2,1)}, u32[]{:S(2)}) copy-start(bf16[1,12,128,128]{3,2,1,0:T(8,128)(2,1)} %param.20) | copy-start | bytes 1179652
  4.6 0.9 %copy-start.3 = (f32[2,256,1,128]{3,2,1,0:T(1,128)S(1)}, f32[2,256,1,128]{3,2,1,0:T(1,128)}, u32[]{:S(2)}) copy-start(f32[2,256,1,128]{3,2,1,0:T(1,128)} %param.17) | copy-start | bytes 786436
  5.5 0.9 %copy-start.4 = (f32[2,256,1,128]{3,2,1,0:T(1,128)S(1)}, f32[2,256,1,128]{3,2,1,0:T(1,128)}, u32[]{:S(2)}) copy-start(f32[2,256,1,128]{3,2,1,0:T(1,128)} %param.18) | copy-start | bytes 786436
  6.5 0.9 %copy-start.5 = (bf16[2,256,256]{2,1,0:T(8,128)(2,1)S(1)}, bf16[2,256,256]{2,1,0:T(8,128)(2,1)}, u32[]{:S(2)}) copy-start(bf16[2,256,256]{2,1,0:T(8,128)(2,1)} %constant.22.clone.rest_4_) | copy-start | bytes 786436
  7.4 0.9 %copy-start.6 = (bf16[2,256,256]{2,1,0:T(8,128)(2,1)S(1)}, bf16[2,256,256]{2,1,0:T(8,128)(2,1)}, u32[]{:S(2)}) copy-start(bf16[2,256,256]{2,1,0:T(8,128)(2,1)} %constant.20.clone.rest_2_) | copy-start | bytes 786436
  8.4 0.9 %copy-start.7 = (bf16[2,256,256]{2,1,0:T(8,128)(2,1)S(1)}, bf16[2,256,256]{2,1,0:T(8,128)(2,1)}, u32[]{:S(2)}) copy-start(bf16[2,256,256]{2,1,0:T(8,128)(2,1)} %constant.19.clone.rest_1_) | copy-start | bytes 786436
  9.3 0.9 %copy-start.8 = (bf16[2,256,256]{2,1,0:T(8,128)(2,1)S(1)}, bf16[2,256,256]{2,1,0:T(8,128)(2,1)}, u32[]{:S(2)}) copy-start(bf16[2,256,256]{2,1,0:T(8,128)(2,1)} %constant.18.clone.rest_0_) | copy-start | bytes 786436
  10.3 0.9 %copy-start.9 = (f32[2,128,128]{2,1,0:T(8,128)S(1)}, f32[2,128,128]{2,1,0:T(8,128)}, u32[]{:S(2)}) copy-start(f32[2,128,128]{2,1,0:T(8,128)} %probe.1) | copy-start | bytes 393220
  11.2 0.9 %copy-start.10 = (bf16[256,256]{1,0:T(8,128)(2,1)S(1)}, bf16[256,256]{1,0:T(8,128)(2,1)}, u32[]{:S(2)}) copy-start(bf16[256,256]{1,0:T(8,128)(2,1)} %constant.21.clone.rest_3_) | copy-start | bytes 393220
  12.1 0.7 %copy-start.11 = (s32[1,12]{1,0:T(1,128)S(1)}, s32[1,12]{1,0:T(1,128)}, u32[]{:S(2)}) copy-start(s32[1,12]{1,0:T(1,128)} %tiles.1) | copy-start | bytes 148
where the time goes:
time: 61.1 us; the launch traced here: 60.6 us
  Pallas kernels  44.8 us (73%)
  local copies, waits for them, and re-layouts  14.5 us (24%)
  between operations  1.31 us (2%)
    pallas_call x1, Pallas kernels, body(): pl.pallas_call(kernel, out_shape=[jax.ShapeDtypeStruct(object_slices.shap...  44.8 us
    unnamed x28, local copies, waits for them, and re-layouts  14.5 us

commit v1 on v0

--- a/solution.py
+++ b/solution.py
@@ -107,7 +107,7 @@
 
 
 def spectrum(obj, t, out):
-    def pair(i, carry):
+    for i in range(SLICE_DEV // 2):
         rows = [jnp.concatenate([obj[0, 2 * i + z], obj[1, 2 * i + z]], axis=1) for z in range(2)]
         high, low = split(jnp.concatenate(rows, axis=0))
         half = dot(high, t["right"][0]) + dot(low, t["right"][0]) + dot(high, t["right"][1])
@@ -120,9 +120,6 @@
                 rows, lanes = slice(c * SIDE, (c + 1) * SIDE), slice(z * SIDE, (z + 1) * SIDE)
                 out[c, 2 * i + z, :, :SIDE] = high[rows, lanes]
                 out[c, 2 * i + z, :, SIDE:] = low[rows, lanes]
-        return carry
-
-    lax.fori_loop(0, SLICE_DEV // 2, pair, 0)
 
 
 def sample(plane, c, t, put):
@@ -178,7 +175,7 @@
 
 
 def correction(grid, t, put):
-    def pair(i, carry):
+    for i in range(SLICE_DEV // 2):
         rows = [jnp.concatenate([grid[0, 2 * i + z], grid[1, 2 * i + z]], axis=1) for z in range(2)]
         half = dot(jnp.concatenate(rows, axis=0), t["left"][0]).astype(BF16)
         cols = jnp.concatenate([stacked(half[:SIDE]), stacked(half[SIDE:])], axis=1)
@@ -186,9 +183,6 @@
         for z in range(2):
             for c in range(2):
                 put(c, 2 * i + z, full[c * SIDE : (c + 1) * SIDE, z * SIDE : (z + 1) * SIDE])
-        return carry
-
-    lax.fori_loop(0, SLICE_DEV // 2, pair, 0)
 
 
 def patches(extended, probe, measured, starts, count, t, grads, probe_grad, power):
@@ -243,15 +237,25 @@
             power[...] = squares
 
 
-def kernel(obj, views, dual, probe, measured, tiles, count, *rest):
-    t = dict(zip(TABLE_NAMES, rest))
-    rest = rest[len(TABLE_NAMES) :]
+LOADED = ["views", "dual", "obj", "probe", "measured"] + TABLE_NAMES
+LOAD_ORDER = ["views", "obj", "right", "left", "probe", "measured", "half", "dual"] + [
+    "across", "along", "to_view", "to_line", "along16", "spread"
+]
+
+
+def kernel(tiles, count, *rest):
+    far = dict(zip(LOADED, rest))
+    rest = rest[len(LOADED) :]
     obj_out, views_out, dual_out, probe_out = rest[:4]
+    rest = rest[4:]
+    near = dict(zip(LOADED[1:], rest))
     (
-        extended, halo, grads, probe_grad, power, grad_out, grad_in, target, spec, lines, back, grid,
+        extended, grads, probe_grad, power, grad_out, grad_in, target, spec, lines, back, grid,
         came, now_send, now_came, after_send, after_came, chunk_send, chunk_came, slab_send, slab_came,
-        halo_sem, grad_sem, target_sem, now_sem, after_sem, chunk_sem, slab_sem, gather_sem,
-    ) = rest[4:]
+        halo_sem, grad_sem, target_sem, now_sem, after_sem, chunk_sem, slab_sem, gather_sem, load_sem,
+    ) = rest[len(LOADED) - 1 :]
+    obj, dual, probe, measured = (near[name] for name in ("obj", "dual", "probe", "measured"))
+    t = near
     slab, ang = lax.axis_index("slab"), lax.axis_index("ang")
 
     def ang_peer(k):
@@ -278,19 +282,31 @@
     def await_bytes(ref, sem):
         pltpu.make_async_copy(ref, ref, sem).wait()
 
+    near["views"] = extended.at[:, :ROWS, :]
+    loads = {}
+    for name in LOAD_ORDER:
+        loads[name] = pltpu.make_async_copy(far[name], near[name], load_sem.at[LOAD_ORDER.index(name)])
     barrier = pltpu.get_barrier_semaphore()
     each_ang(lambda p: pl.semaphore_signal(barrier, inc=1, device_id=(slab, p), device_id_type=MESH))
     for k in range(1, N_SLAB):
         pl.semaphore_signal(barrier, inc=1, device_id=(slab_peer(k), ang), device_id_type=MESH)
+    for name in LOAD_ORDER:
+        loads[name].start()
     pl.semaphore_wait(barrier, ANGLES - 1 + N_SLAB - 1)
 
-    halo_copy = remote(views.at[:, :HALO, :], halo, halo_sem, (slab_peer(N_SLAB - 1), ang))
+    loads["views"].wait()
+    halo_copy = remote(
+        extended.at[:, :HALO, :], extended.at[:, ROWS:, :], halo_sem, (slab_peer(N_SLAB - 1), ang)
+    )
     halo_copy.start()
+    for name in ("obj", "right", "left"):
+        loads[name].wait()
     spectrum(obj, t, spec)
-    extended[:, : ROWS, :] = views[...]
+    for name in ("probe", "measured", "half", "dual"):
+        loads[name].wait()
     halo_copy.wait()
     inner = jnp.where(slab < N_SLAB - 1, 1.0, 0.0).astype(F32)
-    extended[:, ROWS:, :] = halo[...] * inner
+    extended[:, ROWS:, :] = extended[:, ROWS:, :] * inner
 
     picked = [tiles[0, n] for n in range(CAP)]
     starts = [tile * STEP for tile in picked]
@@ -319,7 +335,7 @@
         sums = gathered(r)
         at = pl.ds(pl.multiple_of(r * STEP, STEP), STEP)
         for c in range(2):
-            target[c, at, :] = (1.0 - view_rate) * (views[c, at, :] + dual[c, at, :]) - view_rate * sums[c]
+            target[c, at, :] = (1.0 - view_rate) * (extended[c, at, :] + dual[c, at, :]) - view_rate * sums[c]
         return carry
 
     lax.fori_loop(0, ROWS // STEP, inside, 0)
@@ -342,6 +358,9 @@
     each_ang(lambda p: remote(chunk_send.at[p], chunk_came.at[ang], chunk_sem, (slab, p)).start())
     chunk_came[ang] = chunk_send[ang]
 
+    for name in ("across", "along", "to_view", "to_line", "along16", "spread"):
+        loads[name].wait()
+
     def put_line(c, a, samples):
         lines[c, a] = samples
 
@@ -399,12 +418,11 @@
         obj_out[c, z] = obj[c, z] - value
 
     correction(grid, t, put_object)
-
     await_bytes(block_span(now_came), now_sem.at[1])
     views_out[...] = target[...] - dual[...] + view_rate * now_came[...]
+    await_bytes(probe_out.at[: 8 * (ANGLES - 1), :], gather_sem.at[1])
     await_bytes(block_span(after_came), after_sem.at[1])
     dual_out[...] = target[...] + view_rate * now_came[...] - after_came[...]
-    await_bytes(probe_out.at[: 8 * (ANGLES - 1), :], gather_sem.at[1])
 
     await_bytes(came.at[: ANGLES - 1], target_sem.at[0])
     await_bytes(now_send.at[: ANGLES - 1], now_sem.at[0])
@@ -414,60 +432,77 @@
     await_bytes(probe_out.at[: 8 * (ANGLES - 1), :], gather_sem.at[0])
 
 
+def store_all(*refs):
+    copies = [pltpu.make_async_copy(refs[i], refs[4 + i], refs[8].at[i]) for i in range(4)]
+    for copy in copies:
+        copy.start()
+    for copy in copies:
+        copy.wait()
+
+
 def block_span(ref):
     return ref.at[:, : SLICE_DEV * (ANGLES - 1), :]
 
 
 def body(object_slices, views, scaled_dual, probe, intensities, tile_rows, live_counts):
     table = tables()
-    args = [
-        object_slices,
-        views.reshape(2, ROWS, SIDE),
-        scaled_dual.reshape(2, ROWS, SIDE),
-        probe,
-        intensities.reshape(CAP, SIDE, SIDE),
-        tile_rows,
-        live_counts,
-    ] + [jnp.asarray(table[name]) for name in TABLE_NAMES]
-    vmem, smem = pl.BlockSpec(memory_space=pltpu.VMEM), pl.BlockSpec(memory_space=pltpu.SMEM)
+    arrays = dict(
+        views=views.reshape(2, ROWS, SIDE),
+        dual=scaled_dual.reshape(2, ROWS, SIDE),
+        obj=object_slices,
+        probe=probe,
+        measured=intensities.reshape(CAP, SIDE, SIDE),
+        **{name: jnp.asarray(table[name]) for name in TABLE_NAMES},
+    )
+    far, smem = pl.BlockSpec(memory_space=pltpu.HBM), pl.BlockSpec(memory_space=pltpu.SMEM)
     blocks = (ANGLES, 2, SLICE_DEV, SIDE)
     dma = pltpu.SemaphoreType.DMA((2,))
+    scratch = [pltpu.VMEM(arrays[name].shape, arrays[name].dtype) for name in LOADED[1:]] + [
+        pltpu.VMEM((2, ROWS + HALO, SIDE), F32),
+        pltpu.VMEM((CAP, 2, SIDE + 2 * STEP, SIDE), F32),
+        pltpu.VMEM((2, SIDE, SIDE), F32),
+        pltpu.VMEM((8, SIDE), F32),
+        pltpu.VMEM((2, HALO, SIDE), F32),
+        pltpu.VMEM((2, HALO, SIDE), F32),
+        pltpu.VMEM((2, ROWS, SIDE), F32),
+        pltpu.VMEM((2, SLICE_DEV, SIDE, 2 * SIDE), BF16),
+        pltpu.VMEM((2, ANGLES, SLICE_DEV, SIDE), F32),
+        pltpu.VMEM((2, ANGLES, SLICE_DEV, SIDE), F32),
+        pltpu.VMEM((2, SLICE_DEV, SIDE, SIDE), BF16),
+        pltpu.VMEM(blocks, F32),
+        pltpu.VMEM(blocks, F32),
+        pltpu.VMEM((2, ROWS, SIDE), F32),
+        pltpu.VMEM(blocks, F32),
+        pltpu.VMEM((2, ROWS, SIDE), F32),
+        pltpu.VMEM((ANGLES, 16, SIDE), F32),
+        pltpu.VMEM((ANGLES, 16, SIDE), F32),
+        pltpu.VMEM((16, SIDE), F32),
+        pltpu.VMEM((N_SLAB, 16, SIDE), F32),
+    ]
+    near = pl.BlockSpec(memory_space=pltpu.VMEM)
+    results = [
+        jax.ShapeDtypeStruct(object_slices.shape, F32),
+        jax.ShapeDtypeStruct((2, ROWS, SIDE), F32),
+        jax.ShapeDtypeStruct((2, ROWS, SIDE), F32),
+        jax.ShapeDtypeStruct((2 * SIDE, SIDE), F32),
+    ]
+    made = pl.pallas_call(
+        kernel,
+        out_shape=results,
+        in_specs=[smem] * 2 + [far] * len(LOADED),
+        out_specs=[near] * 4,
+        scratch_shapes=scratch
+        + [dma] * 8
+        + [pltpu.SemaphoreType.DMA((len(LOADED),))],
+        compiler_params=pltpu.CompilerParams(collective_id=0, has_side_effects=True, vmem_limit_bytes=56 * 1024 * 1024),
+    )(tile_rows, live_counts, *[arrays[name] for name in LOADED])
     obj_new, views_new, dual_new, probe_new = pl.pallas_call(
-        kernel,
-        out_shape=[
-            jax.ShapeDtypeStruct(object_slices.shape, F32),
-            jax.ShapeDtypeStruct((2, ROWS, SIDE), F32),
-            jax.ShapeDtypeStruct((2, ROWS, SIDE), F32),
-            jax.ShapeDtypeStruct((2 * SIDE, SIDE), F32),
-        ],
-        in_specs=[vmem] * 5 + [smem] * 2 + [vmem] * len(TABLE_NAMES),
-        out_specs=[vmem] * 4,
-        scratch_shapes=[
-            pltpu.VMEM((2, ROWS + HALO, SIDE), F32),
-            pltpu.VMEM((2, HALO, SIDE), F32),
-            pltpu.VMEM((CAP, 2, SIDE + 2 * STEP, SIDE), F32),
-            pltpu.VMEM((2, SIDE, SIDE), F32),
-            pltpu.VMEM((8, SIDE), F32),
-            pltpu.VMEM((2, HALO, SIDE), F32),
-            pltpu.VMEM((2, HALO, SIDE), F32),
-            pltpu.VMEM((2, ROWS, SIDE), F32),
-            pltpu.VMEM((2, SLICE_DEV, SIDE, 2 * SIDE), BF16),
-            pltpu.VMEM((2, ANGLES, SLICE_DEV, SIDE), F32),
-            pltpu.VMEM((2, ANGLES, SLICE_DEV, SIDE), F32),
-            pltpu.VMEM((2, SLICE_DEV, SIDE, SIDE), BF16),
-            pltpu.VMEM(blocks, F32),
-            pltpu.VMEM(blocks, F32),
-            pltpu.VMEM((2, ROWS, SIDE), F32),
-            pltpu.VMEM(blocks, F32),
-            pltpu.VMEM((2, ROWS, SIDE), F32),
-            pltpu.VMEM((ANGLES, 16, SIDE), F32),
-            pltpu.VMEM((ANGLES, 16, SIDE), F32),
-            pltpu.VMEM((16, SIDE), F32),
-            pltpu.VMEM((N_SLAB, 16, SIDE), F32),
-        ]
-        + [dma] * 8,
-        compiler_params=pltpu.CompilerParams(collective_id=0, has_side_effects=True, vmem_limit_bytes=48 * 1024 * 1024),
-    )(*args)
+        store_all,
+        out_shape=results,
+        in_specs=[near] * 4,
+        out_specs=[far] * 4,
+        scratch_shapes=[pltpu.SemaphoreType.DMA((4,))],
+    )(*made)
     return (
         obj_new,
         views_new.reshape(views.shape),

time: 61.1 us -> 46.7 us (0.76)
  local copies, waits for them, and re-layouts: 14.5 us -> 0 us
    unnamed x28 -> x0, local copies, waits for them, and re-layouts: 14.5 us -> none
    pallas_call x1 -> x2, Pallas kernels: 44.8 us -> 45.3 us  [the longest x1 42.7 us: body(): pl.pallas_call(kernel, out_shape=results, in_specs=[smem] * 2 + [far] * l...]
where the time goes in v1:
time: 46.7 us; the launch traced here: 46.6 us
  Pallas kernels  45.3 us (97%)
  between operations  1.29 us (3%)
    pallas_call x1, Pallas kernels, body(): pl.pallas_call(kernel, out_shape=results, in_specs=[smem] * 2 + [far] * l...  42.7 us
    pallas_call x1, Pallas kernels, body(): pl.pallas_call(store_all, out_shape=results, in_specs=[near] * 4, out_spe...  2.59 us

profile of v1, /device:TPU:1, one launch (start us, length us, event | category | flops | bytes accessed | tf_op | source)
XLA Modules:
  0.0 46.6 jit_solution(14504592980226104066)
XLA Ops:
  1.3 42.7 %shard_map.183 = (f32[2,8,128,128]{3,2,1,0:T(8,128)}, f32[2,256,128]{2,1,0:T(8,128)}, f32[2,256,128]{2,1,0:T(8,128)}, f32[256,128]{1,0:T(8,128)}) custom-call(s32[1,12]{1,0:T(1,128)} %tiles.1, s32[1,1]{1,0:T(1,128)S(6)} %copy.22.count, f32[2,256,128]{2,1,0:T(8,128)} %bitcast.11, f32[2,256,128]{2,1,0:T(8,128)} %bitcast.12, f32[2,8,128,128]{3,2,1,0:T(8,128)} %rest_2_.1, ...), custom_call_target="tpu_custom_call" | custom-call | tf_op jit(solution)/shard_map/pallas_call | solution.py:489
  44.0 2.6 %shard_map.184 = (f32[2,8,128,128]{3,2,1,0:T(8,128)}, f32[2,256,128]{2,1,0:T(8,128)}, f32[2,256,128]{2,1,0:T(8,128)}, f32[256,128]{1,0:T(8,128)}) custom-call(f32[2,8,128,128]{3,2,1,0:T(8,128)} %get-tuple-element.12.refs_0_, f32[2,256,128]{2,1,0:T(8,128)} %get-tuple-element.13.refs_1_, f32[2,256,128]{2,1,0:T(8,128)} %get-tuple-element.14.refs_2_, ...), custom_call_target="tpu_custom_call" | custom-call | tf_op jit(solution)/shard_map/pallas_call | solution.py:499

commit v2 on v1

--- a/solution.py
+++ b/solution.py
@@ -30,6 +30,10 @@
 MESH = pl.DeviceIdType.MESH
 
 GROUPS = [(0, 1), (2, 3), (4, 5), (6, 7), (8, 9), (10, 11), (12, 13), (14, 15), (16,)]
+OFFSETS = sorted(
+    [(x, y, core) for x in range(4) for y in range(4) for core in range(2)][1:],
+    key=lambda o: -(min(o[0], 4 - o[0]) + min(o[1], 4 - o[1])),
+)
 REACH = [16, 32, 32, 48, 64, 64, 64, 64, 64]
 
 
@@ -185,7 +189,7 @@
                 put(c, 2 * i + z, full[c * SIDE : (c + 1) * SIDE, z * SIDE : (z + 1) * SIDE])
 
 
-def patches(extended, probe, measured, starts, count, t, grads, probe_grad, power):
+def patches(extended, probe, measured, starts, count, t, grads, chunks, power):
     probe_re, probe_im = probe[0], probe[1]
     edge = jnp.zeros((2, STEP, SIDE), F32)
     for first in range(0, CAP, BATCH):
@@ -227,14 +231,10 @@
             sum_re = term_re if sum_re is None else sum_re + term_re
             sum_im = term_im if sum_im is None else sum_im + term_im
             squares = square if squares is None else squares + square
-        if first:
-            probe_grad[0] += sum_re
-            probe_grad[1] += sum_im
-            power[...] += squares
-        else:
-            probe_grad[0] = sum_re
-            probe_grad[1] = sum_im
-            power[...] = squares
+        for i in range(ANGLES):
+            part = (sum_re, sum_im)[i // 16][(i % 16) * 8 : (i % 16 + 1) * 8]
+            chunks[i] = chunks[i] + part if first else part
+        power[...] = power[...] + squares if first else squares
 
 
 LOADED = ["views", "dual", "obj", "probe", "measured"] + TABLE_NAMES
@@ -250,26 +250,25 @@
     rest = rest[4:]
     near = dict(zip(LOADED[1:], rest))
     (
-        extended, grads, probe_grad, power, grad_out, grad_in, target, spec, lines, back, grid,
-        came, now_send, now_came, after_send, after_came, chunk_send, chunk_came, slab_send, slab_came,
-        halo_sem, grad_sem, target_sem, now_sem, after_sem, chunk_sem, slab_sem, gather_sem, load_sem,
+        extended, grads, chunks, power, grad_out, grad_in, target, spec, lines, back, grid,
+        came, now_send, now_came, after_send, after_came, chunks_came, slabs, gathered_rows,
+        halo_sem, grad_sem, target_sem, now_sem, after_sem, chunk_sem, slab_sem, row_sem, load_sem,
     ) = rest[len(LOADED) - 1 :]
     obj, dual, probe, measured = (near[name] for name in ("obj", "dual", "probe", "measured"))
     t = near
     slab, ang = lax.axis_index("slab"), lax.axis_index("ang")
 
-    def ang_peer(k):
-        return lax.rem(ang + k, ANGLES)
-
     def slab_peer(k):
         return lax.rem(slab + k, N_SLAB)
 
+    across_x, across_y, core = ang // 8, lax.rem(ang // 2, 4), lax.rem(ang, 2)
+    others = [
+        lax.rem(across_x + x, 4) * 8 + lax.rem(across_y + y, 4) * 2 + lax.rem(core + c, 2) for x, y, c in OFFSETS
+    ]
+
     def each_ang(body):
-        def step(k, carry):
-            body(ang_peer(k))
-            return carry
-
-        lax.fori_loop(1, ANGLES, step, 0)
+        for p in others:
+            body(p)
 
     def remote(src, dst, sems, to):
         return pltpu.make_async_remote_copy(
@@ -298,19 +297,23 @@
     halo_copy = remote(
         extended.at[:, :HALO, :], extended.at[:, ROWS:, :], halo_sem, (slab_peer(N_SLAB - 1), ang)
     )
-    halo_copy.start()
+    pl.when(slab > 0)(halo_copy.start)
     for name in ("obj", "right", "left"):
         loads[name].wait()
     spectrum(obj, t, spec)
     for name in ("probe", "measured", "half", "dual"):
         loads[name].wait()
-    halo_copy.wait()
-    inner = jnp.where(slab < N_SLAB - 1, 1.0, 0.0).astype(F32)
-    extended[:, ROWS:, :] = extended[:, ROWS:, :] * inner
+    pl.when(slab < N_SLAB - 1)(halo_copy.wait_recv)
+
+    @pl.when(slab == N_SLAB - 1)
+    def _():
+        extended[:, ROWS:, :] = jnp.zeros((2, HALO, SIDE), F32)
 
     picked = [tiles[0, n] for n in range(CAP)]
     starts = [tile * STEP for tile in picked]
-    patches(extended, probe, measured, starts, count[0, 0], t, grads, probe_grad, power)
+    patches(extended, probe, measured, starts, count[0, 0], t, grads, chunks, power)
+    each_ang(lambda p: remote(chunks.at[p], chunks_came.at[ang], chunk_sem, (slab, p)).start())
+    chunks_came[ang] = chunks[ang]
 
     def gathered(r):
         sums = [None, None]
@@ -329,7 +332,7 @@
 
     lax.fori_loop(0, HALO // STEP, outer, 0)
     grad_copy = remote(grad_out, grad_in, grad_sem, (slab_peer(1), ang))
-    grad_copy.start()
+    pl.when(slab < N_SLAB - 1)(grad_copy.start)
 
     def inside(r, carry):
         sums = gathered(r)
@@ -346,17 +349,13 @@
     ready = HALO // SLICE_DEV
     each_ang(lambda p: pl.when(p >= ready)(lambda: send_target(p)))
 
-    for c in range(2):
-        for i in range(SIDE // 8):
-            chunk_send[c * (SIDE // 8) + i, :8, :] = probe_grad[c, 8 * i : 8 * i + 8, :]
-            chunk_send[c * (SIDE // 8) + i, 8:, :] = power[...]
-    grad_copy.wait()
-    from_above = jnp.where(slab > 0, view_rate, 0.0).astype(F32)
-    target[:, :HALO, :] = target[:, :HALO, :] - from_above * grad_in[...]
+    @pl.when(slab > 0)
+    def _():
+        grad_copy.wait_recv()
+        target[:, :HALO, :] = target[:, :HALO, :] - view_rate * grad_in[...]
+
     each_ang(lambda p: pl.when(p < ready)(lambda: send_target(p)))
     came[ang] = target[:, pl.ds(pl.multiple_of(ang * SLICE_DEV, SLICE_DEV), SLICE_DEV), :]
-    each_ang(lambda p: remote(chunk_send.at[p], chunk_came.at[ang], chunk_sem, (slab, p)).start())
-    chunk_came[ang] = chunk_send[ang]
 
     for name in ("across", "along", "to_view", "to_line", "along16", "spread"):
         loads[name].wait()
@@ -374,17 +373,15 @@
         now_send[:, c] = value
 
     lines_to_views(lines, t, put_now)
+    await_bytes(chunks_came.at[: ANGLES - 1], chunk_sem.at[1])
+    slabs[slab, :8, :] = jnp.sum(chunks_came[...], axis=0)
+    slabs[slab, 8:, :] = power[...]
+    for k in range(1, N_SLAB):
+        remote(slabs.at[slab], slabs.at[slab], slab_sem, (slab_peer(k), ang)).start()
+
+    await_bytes(came.at[: ANGLES - 1], target_sem.at[1])
     each_ang(lambda p: remote(now_send.at[p], block(now_came, ang), now_sem, (slab, p)).start())
     now_came[:, pl.ds(pl.multiple_of(ang * SLICE_DEV, SLICE_DEV), SLICE_DEV), :] = now_send[ang]
-
-    await_bytes(chunk_came.at[: ANGLES - 1], chunk_sem.at[1])
-    total = jnp.sum(chunk_came[...], axis=0)
-    slab_send[...] = total
-    for k in range(1, N_SLAB):
-        remote(slab_send, slab_came.at[slab], slab_sem, (slab_peer(k), ang)).start()
-    slab_came[slab] = total
-
-    await_bytes(came.at[: ANGLES - 1], target_sem.at[1])
     joined = jnp.concatenate([came[:, c].reshape(ROWS, SIDE) for c in range(2)], axis=1).astype(BF16)
     pulled = dot(joined, t["to_line"][...])
     for c in range(2):
@@ -393,11 +390,18 @@
     def put_after(c, a, samples):
         lines[c, a] = lines[c, a] - samples * (1.0 / ANGLES)
 
+    def spread_back(c, carry):
+        spread(back, c, t, grid)
+        return carry
+
     def sample_after(c, carry):
-        spread(back, c, t, grid)
         sample(grid, c, t, put_after)
         return carry
 
+    lax.fori_loop(0, 2, spread_back, 0)
+    await_bytes(slabs.at[: N_SLAB - 1], slab_sem.at[1])
+    gathered_rows[ang] = jnp.sum(slabs[...], axis=0)
+    each_ang(lambda p: remote(gathered_rows.at[ang], gathered_rows.at[ang], row_sem, (slab, p)).start())
     lax.fori_loop(0, 2, sample_after, 0)
 
     def put_views(c, value):
@@ -407,29 +411,28 @@
     each_ang(lambda p: remote(after_send.at[p], block(after_came, ang), after_sem, (slab, p)).start())
     after_came[:, pl.ds(pl.multiple_of(ang * SLICE_DEV, SLICE_DEV), SLICE_DEV), :] = after_send[ang]
 
-    await_bytes(slab_came.at[: N_SLAB - 1], slab_sem.at[1])
-    total = jnp.sum(slab_came[...], axis=0)
-    scale = probe_rate / (jnp.sum(total[8:]) * (1.0 / (SIDE * SIDE)) + epsilon)
-    mine = pl.ds(pl.multiple_of(ang * 8, 8), 8)
-    probe_out[mine, :] = probe.reshape(2 * SIDE, SIDE)[mine, :] - total[:8] * scale
-    each_ang(lambda p: remote(probe_out.at[mine, :], probe_out.at[mine, :], gather_sem, (slab, p)).start())
-
     def put_object(c, z, value):
         obj_out[c, z] = obj[c, z] - value
 
     correction(grid, t, put_object)
     await_bytes(block_span(now_came), now_sem.at[1])
     views_out[...] = target[...] - dual[...] + view_rate * now_came[...]
-    await_bytes(probe_out.at[: 8 * (ANGLES - 1), :], gather_sem.at[1])
+    await_bytes(gathered_rows.at[: ANGLES - 1], row_sem.at[1])
+    scale = probe_rate / (jnp.sum(gathered_rows[:, 8:, :]) * (1.0 / (SIDE * SIDE)) + epsilon)
+    for c in range(2):
+        rows = gathered_rows[c * 16 : (c + 1) * 16, :8, :].reshape(SIDE, SIDE)
+        probe_out[c] = probe[c] - rows * scale
     await_bytes(block_span(after_came), after_sem.at[1])
     dual_out[...] = target[...] + view_rate * now_came[...] - after_came[...]
 
     await_bytes(came.at[: ANGLES - 1], target_sem.at[0])
     await_bytes(now_send.at[: ANGLES - 1], now_sem.at[0])
     await_bytes(after_send.at[: ANGLES - 1], after_sem.at[0])
-    await_bytes(chunk_send.at[: ANGLES - 1], chunk_sem.at[0])
-    await_bytes(slab_came.at[: N_SLAB - 1], slab_sem.at[0])
-    await_bytes(probe_out.at[: 8 * (ANGLES - 1), :], gather_sem.at[0])
+    await_bytes(chunks_came.at[: ANGLES - 1], chunk_sem.at[0])
+    await_bytes(slabs.at[: N_SLAB - 1], slab_sem.at[0])
+    await_bytes(gathered_rows.at[: ANGLES - 1], row_sem.at[0])
+    pl.when(slab > 0)(halo_copy.wait_send)
+    pl.when(slab < N_SLAB - 1)(grad_copy.wait_send)
 
 
 def store_all(*refs):
@@ -460,7 +463,7 @@
     scratch = [pltpu.VMEM(arrays[name].shape, arrays[name].dtype) for name in LOADED[1:]] + [
         pltpu.VMEM((2, ROWS + HALO, SIDE), F32),
         pltpu.VMEM((CAP, 2, SIDE + 2 * STEP, SIDE), F32),
-        pltpu.VMEM((2, SIDE, SIDE), F32),
+        pltpu.VMEM((ANGLES, 8, SIDE), F32),
         pltpu.VMEM((8, SIDE), F32),
         pltpu.VMEM((2, HALO, SIDE), F32),
         pltpu.VMEM((2, HALO, SIDE), F32),
@@ -474,17 +477,16 @@
         pltpu.VMEM((2, ROWS, SIDE), F32),
         pltpu.VMEM(blocks, F32),
         pltpu.VMEM((2, ROWS, SIDE), F32),
+        pltpu.VMEM((ANGLES, 8, SIDE), F32),
+        pltpu.VMEM((N_SLAB, 16, SIDE), F32),
         pltpu.VMEM((ANGLES, 16, SIDE), F32),
-        pltpu.VMEM((ANGLES, 16, SIDE), F32),
-        pltpu.VMEM((16, SIDE), F32),
-        pltpu.VMEM((N_SLAB, 16, SIDE), F32),
     ]
     near = pl.BlockSpec(memory_space=pltpu.VMEM)
     results = [
         jax.ShapeDtypeStruct(object_slices.shape, F32),
         jax.ShapeDtypeStruct((2, ROWS, SIDE), F32),
         jax.ShapeDtypeStruct((2, ROWS, SIDE), F32),
-        jax.ShapeDtypeStruct((2 * SIDE, SIDE), F32),
+        jax.ShapeDtypeStruct(probe.shape, F32),
     ]
     made = pl.pallas_call(
         kernel,
@@ -507,7 +509,7 @@
         obj_new,
         views_new.reshape(views.shape),
         dual_new.reshape(scaled_dual.shape),
-        probe_new.reshape(probe.shape),
+        probe_new,
     )
 
 

time: 46.7 us -> 41.8 us (0.90)
  Pallas kernels: 45.3 us -> 40.3 us
    pallas_call x1, Pallas kernels: 42.7 us -> 37.8 us  [body(): pl.pallas_call(kernel, out_shape=results, in_specs=[smem] * 2 + [far] * l...]
where the time goes in v2:
time: 41.8 us; the launch traced here: 41.6 us
  Pallas kernels  40.3 us (96%)
  between operations  1.29 us (3%)
    pallas_call x1, Pallas kernels, body(): pl.pallas_call(kernel, out_shape=results, in_specs=[smem] * 2 + [far] * l...  37.8 us
    pallas_call x1, Pallas kernels, body(): pl.pallas_call(store_all, out_shape=results, in_specs=[near] * 4, out_spe...  2.59 us

profile of v2, /device:TPU:1, one launch (start us, length us, event | category | flops | bytes accessed | tf_op | source)
XLA Modules:
  0.0 41.6 jit_solution(13732177165804009525)
XLA Ops:
  1.3 37.8 %shard_map.183 = (f32[2,8,128,128]{3,2,1,0:T(8,128)}, f32[2,256,128]{2,1,0:T(8,128)}, f32[2,256,128]{2,1,0:T(8,128)}, f32[2,128,128]{2,1,0:T(8,128)}) custom-call(s32[1,12]{1,0:T(1,128)} %tiles.1, s32[1,1]{1,0:T(1,128)S(6)} %copy.22.count, f32[2,256,128]{2,1,0:T(8,128)} %bitcast.10, f32[2,256,128]{2,1,0:T(8,128)} %bitcast.11, f32[2,8,128,128]{3,2,1,0:T(8,128)} %rest_2_.1, ...), custom_call_target="tpu_custom_call" | custom-call | tf_op jit(solution)/shard_map/pallas_call | solution.py:491
  39.0 2.6 %shard_map.184 = (f32[2,8,128,128]{3,2,1,0:T(8,128)}, f32[2,256,128]{2,1,0:T(8,128)}, f32[2,256,128]{2,1,0:T(8,128)}, f32[2,128,128]{2,1,0:T(8,128)}) custom-call(f32[2,8,128,128]{3,2,1,0:T(8,128)} %get-tuple-element.12.refs_0_, f32[2,256,128]{2,1,0:T(8,128)} %get-tuple-element.13.refs_1_, f32[2,256,128]{2,1,0:T(8,128)} %get-tuple-element.14.refs_2_, ...), custom_call_target="tpu_custom_call" | custom-call | tf_op jit(solution)/shard_map/pallas_call | solution.py:501

commit v3 on v2

--- a/solution.py
+++ b/solution.py
@@ -35,6 +35,10 @@
     key=lambda o: -(min(o[0], 4 - o[0]) + min(o[1], 4 - o[1])),
 )
 REACH = [16, 32, 32, 48, 64, 64, 64, 64, 64]
+
+SAMPLE_BATCH = {16: 4, 32: 4, 48: 4, 64: 4}
+SPREAD_BATCH = 4
+EARLY, LATE = (8, 7, 5, 3, 1), (6, 4, 2, 0)
 
 
 def dft_tables():
@@ -126,17 +130,21 @@
                 out[c, 2 * i + z, :, SIDE:] = low[rows, lanes]
 
 
-def sample(plane, c, t, put):
+def sample(plane, c, t, put, groups):
     depth = plane.shape[-1]
-    for g, members in enumerate(GROUPS):
+    for g in groups:
+        members = GROUPS[g]
         lanes = len(members) * SIDE
         low, top = HALF - REACH[g], HALF + REACH[g]
+        batch = SAMPLE_BATCH[REACH[g]]
         sums = [[], []]
-        for z in range(SLICE_DEV):
-            rows = dot(plane[c, z, low:top, :], t["across"][g, :depth, :lanes])
+        for first in range(0, SLICE_DEV, batch):
+            rows = plane[c, first : first + batch, low:top, :].reshape(batch * (top - low), depth)
+            rows = dot(rows, t["across"][g, :depth, :lanes]).reshape(batch, top - low, lanes)
             for side in range(len(members)):
-                weighed = rows * t["along"][g, side, low:top, :lanes]
-                sums[side].append(jnp.sum(weighed, axis=0, keepdims=True))
+                weight = t["along"][g, side, low:top, :lanes]
+                for z in range(batch):
+                    sums[side].append(jnp.sum(rows[z] * weight, axis=0, keepdims=True))
         for side in range(len(members)):
             whole = jnp.concatenate(sums[side], axis=0)
             for i, b in enumerate(members):
@@ -145,37 +153,50 @@
 
 
 def spread(lines, c, t, out):
-    for z in range(SLICE_DEV):
-        total = None
+    for first in range(0, SLICE_DEV, SPREAD_BATCH):
+        totals = [None] * SPREAD_BATCH
         for g, members in enumerate(GROUPS):
             lanes = len(members) * SIDE
             low, top = HALF - REACH[g], HALF + REACH[g]
-            terms = None
-            for side in range(len(members)):
-                picks = [lines[c, (QUARTER - b) if side == 0 else (QUARTER + b), z : z + 1, :] for b in members]
-                line = jnp.concatenate(picks, axis=1).astype(BF16)
-                term = t["along16"][g, side, low:top, :lanes] * line
-                terms = term if terms is None else terms + term
-            part = dot(terms, t["spread"][g, :lanes, :])
-            if total is None:
-                total = part
-            else:
-                edge = (part.shape[0] - total.shape[0]) // 2
-                if edge:
-                    total = jnp.concatenate(
-                        [part[:edge], part[edge : edge + total.shape[0]] + total, part[edge + total.shape[0] :]], axis=0
-                    )
-                else:
-                    total = part + total
-        out[c, z] = total.astype(BF16)
-
-
-def lines_to_views(lines, t, put):
-    joined = jnp.concatenate([lines[0].reshape(ROWS, SIDE), lines[1].reshape(ROWS, SIDE)], axis=1)
+            batch = []
+            for z in range(first, first + SPREAD_BATCH):
+                terms = None
+                for side in range(len(members)):
+                    picks = [lines[c, (QUARTER - b) if side == 0 else (QUARTER + b), z : z + 1, :] for b in members]
+                    line = jnp.concatenate(picks, axis=1).astype(BF16)
+                    term = t["along16"][g, side, low:top, :lanes] * line
+                    terms = term if terms is None else terms + term
+                batch.append(terms)
+            parts = dot(jnp.concatenate(batch, axis=0), t["spread"][g, :lanes, :])
+            for i in range(SPREAD_BATCH):
+                part, total = parts[i * (top - low) : (i + 1) * (top - low)], totals[i]
+                if total is not None:
+                    edge = (part.shape[0] - total.shape[0]) // 2
+                    inner = part[edge : edge + total.shape[0]] + total
+                    part = jnp.concatenate([part[:edge], inner, part[edge + total.shape[0] :]], axis=0) if edge else inner
+                totals[i] = part
+        for i in range(SPREAD_BATCH):
+            out[c, first + i] = totals[i].astype(BF16)
+
+
+def angles_of(groups):
+    members = [b for g in groups for b in GROUPS[g]]
+    return sorted({QUARTER - b for b in members} | {QUARTER + b for b in members if b < QUARTER})
+
+
+def is_early(p):
+    below = (p < QUARTER) & (lax.rem((ANGLES + QUARTER - p) // 2, 2) == 1)
+    above = (p >= QUARTER) & (lax.rem((p + QUARTER) // 2, 2) == 1)
+    return below | above | (p == 0)
+
+
+def lines_to_views(lines, t, angles, out):
+    joined = jnp.concatenate([jnp.concatenate([lines[c, a] for a in angles], axis=0) for c in range(2)], axis=1)
     high, low = split(joined)
     result = dot(high, t["to_view"][0]) + dot(low, t["to_view"][0]) + dot(high, t["to_view"][1])
-    for c in range(2):
-        put(c, result[:, c * SIDE : (c + 1) * SIDE].reshape(ANGLES, SLICE_DEV, SIDE))
+    for i, a in enumerate(angles):
+        for c in range(2):
+            out[a, c] = result[i * SLICE_DEV : (i + 1) * SLICE_DEV, c * SIDE : (c + 1) * SIDE]
 
 
 def correction(grid, t, put):
@@ -363,21 +384,21 @@
     def put_line(c, a, samples):
         lines[c, a] = samples
 
-    def sample_now(c, carry):
-        sample(spec, c, t, put_line)
-        return carry
-
-    lax.fori_loop(0, 2, sample_now, 0)
-
-    def put_now(c, value):
-        now_send[:, c] = value
-
-    lines_to_views(lines, t, put_now)
+    def sample_now(groups):
+        def plane(c, carry):
+            sample(spec, c, t, put_line, groups)
+            return carry
+
+        lax.fori_loop(0, 2, plane, 0)
+
+    sample_now(EARLY)
     await_bytes(chunks_came.at[: ANGLES - 1], chunk_sem.at[1])
     slabs[slab, :8, :] = jnp.sum(chunks_came[...], axis=0)
     slabs[slab, 8:, :] = power[...]
     for k in range(1, N_SLAB):
         remote(slabs.at[slab], slabs.at[slab], slab_sem, (slab_peer(k), ang)).start()
+    sample_now(LATE)
+    lines_to_views(lines, t, range(ANGLES), now_send)
 
     await_bytes(came.at[: ANGLES - 1], target_sem.at[1])
     each_ang(lambda p: remote(now_send.at[p], block(now_came, ang), now_sem, (slab, p)).start())
@@ -394,21 +415,25 @@
         spread(back, c, t, grid)
         return carry
 
-    def sample_after(c, carry):
-        sample(grid, c, t, put_after)
-        return carry
+    def sample_after(groups):
+        def plane(c, carry):
+            sample(grid, c, t, put_after, groups)
+            return carry
+
+        lax.fori_loop(0, 2, plane, 0)
+        lines_to_views(lines, t, angles_of(groups), after_send)
+
+    def send_after(p):
+        remote(after_send.at[p], block(after_came, ang), after_sem, (slab, p)).start()
 
     lax.fori_loop(0, 2, spread_back, 0)
     await_bytes(slabs.at[: N_SLAB - 1], slab_sem.at[1])
     gathered_rows[ang] = jnp.sum(slabs[...], axis=0)
     each_ang(lambda p: remote(gathered_rows.at[ang], gathered_rows.at[ang], row_sem, (slab, p)).start())
-    lax.fori_loop(0, 2, sample_after, 0)
-
-    def put_views(c, value):
-        after_send[:, c] = value
-
-    lines_to_views(lines, t, put_views)
-    each_ang(lambda p: remote(after_send.at[p], block(after_came, ang), after_sem, (slab, p)).start())
+    sample_after(EARLY)
+    each_ang(lambda p: pl.when(is_early(p))(lambda: send_after(p)))
+    sample_after(LATE)
+    each_ang(lambda p: pl.when(jnp.logical_not(is_early(p)))(lambda: send_after(p)))
     after_came[:, pl.ds(pl.multiple_of(ang * SLICE_DEV, SLICE_DEV), SLICE_DEV), :] = after_send[ang]
 
     def put_object(c, z, value):

time: 41.8 us -> 39.3 us (0.940)
  Pallas kernels: 40.3 us -> 37.9 us
    pallas_call x1, Pallas kernels: 37.8 us -> 35.3 us  [body(): pl.pallas_call(kernel, out_shape=results, in_specs=[smem] * 2 + [far] * l...]
where the time goes in v3:
time: 39.3 us; the launch traced here: 39.2 us
  Pallas kernels  37.9 us (96%)
  between operations  1.29 us (3%)
    pallas_call x1, Pallas kernels, body(): pl.pallas_call(kernel, out_shape=results, in_specs=[smem] * 2 + [far] * l...  35.3 us
    pallas_call x1, Pallas kernels, body(): pl.pallas_call(store_all, out_shape=results, in_specs=[near] * 4, out_spe...  2.59 us

profile of v3, /device:TPU:1, one launch (start us, length us, event | category | flops | bytes accessed | tf_op | source)
XLA Modules:
  0.0 39.2 jit_solution(8816018205674857795)
XLA Ops:
  1.3 35.3 %shard_map.183 = (f32[2,8,128,128]{3,2,1,0:T(8,128)}, f32[2,256,128]{2,1,0:T(8,128)}, f32[2,256,128]{2,1,0:T(8,128)}, f32[2,128,128]{2,1,0:T(8,128)}) custom-call(s32[1,12]{1,0:T(1,128)} %tiles.1, s32[1,1]{1,0:T(1,128)S(6)} %copy.22.count, f32[2,256,128]{2,1,0:T(8,128)} %bitcast.10, f32[2,256,128]{2,1,0:T(8,128)} %bitcast.11, f32[2,8,128,128]{3,2,1,0:T(8,128)} %rest_2_.1, ...), custom_call_target="tpu_custom_call" | custom-call | tf_op jit(solution)/shard_map/pallas_call | solution.py:516
  36.6 2.6 %shard_map.184 = (f32[2,8,128,128]{3,2,1,0:T(8,128)}, f32[2,256,128]{2,1,0:T(8,128)}, f32[2,256,128]{2,1,0:T(8,128)}, f32[2,128,128]{2,1,0:T(8,128)}) custom-call(f32[2,8,128,128]{3,2,1,0:T(8,128)} %get-tuple-element.12.refs_0_, f32[2,256,128]{2,1,0:T(8,128)} %get-tuple-element.13.refs_1_, f32[2,256,128]{2,1,0:T(8,128)} %get-tuple-element.14.refs_2_, ...), custom_call_target="tpu_custom_call" | custom-call | tf_op jit(solution)/shard_map/pallas_call | solution.py:526

commit v4 on v3

--- a/solution.py
+++ b/solution.py
@@ -16,7 +16,7 @@
 SLICE_DEV = 8
 ROWS = ANGLES * SLICE_DEV
 CAP = 12
-BATCH = 4
+BATCH = 6
 HALO = SIDE - STEP
 N_SLAB = 4
 QUARTER = ANGLES // 2
@@ -38,7 +38,7 @@
 
 SAMPLE_BATCH = {16: 4, 32: 4, 48: 4, 64: 4}
 SPREAD_BATCH = 4
-EARLY, LATE = (8, 7, 5, 3, 1), (6, 4, 2, 0)
+EARLY, LATE = (8, 7, 6, 5, 3, 1), (4, 2, 0)
 
 
 def dft_tables():
@@ -187,7 +187,7 @@
 def is_early(p):
     below = (p < QUARTER) & (lax.rem((ANGLES + QUARTER - p) // 2, 2) == 1)
     above = (p >= QUARTER) & (lax.rem((p + QUARTER) // 2, 2) == 1)
-    return below | above | (p == 0)
+    return below | above | (p <= 4) | (p >= 28)
 
 
 def lines_to_views(lines, t, angles, out):
@@ -400,9 +400,9 @@
     sample_now(LATE)
     lines_to_views(lines, t, range(ANGLES), now_send)
 
-    await_bytes(came.at[: ANGLES - 1], target_sem.at[1])
     each_ang(lambda p: remote(now_send.at[p], block(now_came, ang), now_sem, (slab, p)).start())
     now_came[:, pl.ds(pl.multiple_of(ang * SLICE_DEV, SLICE_DEV), SLICE_DEV), :] = now_send[ang]
+    await_bytes(came.at[: ANGLES - 1], target_sem.at[1])
     joined = jnp.concatenate([came[:, c].reshape(ROWS, SIDE) for c in range(2)], axis=1).astype(BF16)
     pulled = dot(joined, t["to_line"][...])
     for c in range(2):

time: 39.3 us -> 39.3 us (level)
  no operation moved by 1% of the time
where the time goes in v4:
time: 39.3 us; the launch traced here: 39.2 us
  Pallas kernels  37.9 us (96%)
  between operations  1.29 us (3%)
    pallas_call x1, Pallas kernels, body(): pl.pallas_call(kernel, out_shape=results, in_specs=[smem] * 2 + [far] * l...  35.3 us
    pallas_call x1, Pallas kernels, body(): pl.pallas_call(store_all, out_shape=results, in_specs=[near] * 4, out_spe...  2.59 us

profile of v4, /device:TPU:1, one launch (start us, length us, event | category | flops | bytes accessed | tf_op | source)
XLA Modules:
  0.0 39.2 jit_solution(4289184493822540866)
XLA Ops:
  1.3 35.3 %shard_map.183 = (f32[2,8,128,128]{3,2,1,0:T(8,128)}, f32[2,256,128]{2,1,0:T(8,128)}, f32[2,256,128]{2,1,0:T(8,128)}, f32[2,128,128]{2,1,0:T(8,128)}) custom-call(s32[1,12]{1,0:T(1,128)} %tiles.1, s32[1,1]{1,0:T(1,128)S(6)} %copy.22.count, f32[2,256,128]{2,1,0:T(8,128)} %bitcast.10, f32[2,256,128]{2,1,0:T(8,128)} %bitcast.11, f32[2,8,128,128]{3,2,1,0:T(8,128)} %rest_2_.1, ...), custom_call_target="tpu_custom_call" | custom-call | tf_op jit(solution)/shard_map/pallas_call | solution.py:516
  36.6 2.6 %shard_map.184 = (f32[2,8,128,128]{3,2,1,0:T(8,128)}, f32[2,256,128]{2,1,0:T(8,128)}, f32[2,256,128]{2,1,0:T(8,128)}, f32[2,128,128]{2,1,0:T(8,128)}) custom-call(f32[2,8,128,128]{3,2,1,0:T(8,128)} %get-tuple-element.12.refs_0_, f32[2,256,128]{2,1,0:T(8,128)} %get-tuple-element.13.refs_1_, f32[2,256,128]{2,1,0:T(8,128)} %get-tuple-element.14.refs_2_, ...), custom_call_target="tpu_custom_call" | custom-call | tf_op jit(solution)/shard_map/pallas_call | solution.py:526
